TPU v7x, 32 devices: a whole 2x2x4 slice. The times are simulated.
32 devices in a mesh: groups: 2 (over y), learner: 4 (over x, core), tensor: 4 (over z).
Axes of the slice: x: 2, y: 2, z: 4, core: 2. Of those that a mesh axis runs over, the one named last changes fastest.
Arguments:
- hidden: bfloat16 [2, 64, 5120], P(None, ('groups', 'learner')), parts along dimension 1, may hold values from -6 to 6
- input_norm_gain: bfloat16 [5120], replicated, may hold values from 0.5 to 2
- lengths: int32 [64], P(('groups', 'learner')), parts along dimension 0, may hold values from 1 to 1024, as said below
- key_value_cache: bfloat16 [2, 64, 1024, 1024], P(None, ('groups', 'learner'), 'tensor'), parts along dimension 1, may hold values from -512 to 512
- query_base_weight: bfloat16 [5120, 4096], P(None, 'tensor'), may hold values from -0.078125 to 0.078125
- key_value_weight: bfloat16 [2, 5120, 1024], P(None, None, 'tensor'), may hold values from -0.078125 to 0.078125
- output_weight: bfloat16 [4096, 5120], P('tensor'), may hold values from -0.09375 to 0.09375
- adapter_down: bfloat16 [10240, 192], P(('groups', 'learner', 'tensor')), parts along dimension 0, may hold values from -0.078125 to 0.078125
- query_up_factor: bfloat16 [128, 4096], P(('groups', 'learner'), 'tensor'), parts along dimension 0, may hold values from -0.375 to 0.375
- key_value_up: bfloat16 [2, 128, 1024], P(None, ('groups', 'learner'), 'tensor'), parts along dimension 1, may hold values from -0.375 to 0.375
Outputs:
- attended: bfloat16 [2, 64, 5120], P(None, ('groups', 'learner')), parts along dimension 1
- merged_query_weight: bfloat16 [10240, 4096], P('groups', 'tensor'), parts along dimension 0
- kv_merged: bfloat16 [2, 10240, 1024], P(None, 'groups', 'tensor'), parts along dimension 1
There are 2 independent parts, one for each index of `groups`. A program takes and returns all parts, laid end to end along the dimension named above; an argument that names none is the same for every part. Nothing has to cross between parts.
Inputs may be any that keep to these rules, and one draw needn't show every extreme that they name: Row r attends to cache positions below lengths[r]; in every draw some row has exactly 1024.
All inputs are finite; a program needn't handle non-finite values.
Results may differ from a plain program's by a relative error of at most 0.0055.
The roundings to bfloat16 on the way count: a program that leaves them out, or rounds other values in their place, can miss the bound.
Values may be sent and summed in bfloat16 or wider, within the bound.
A program may use at most 192 MiB of HBM per device.

v0:
```python
import jax
import jax.numpy as jnp
from jax import lax
from jax.sharding import PartitionSpec as P

QUERY_HEADS = 32
KEY_VALUE_HEADS = 8
HEAD_DIM = 128


ADAPTER_SCALE = 2.0
ROPE_BASE = 1000000.0
MASKED_SCORE = -1e30
NORM_EPSILON = 1e-06


def joined(part, axis, combine):
    gathered = jax.tree.map(lambda a: lax.all_gather(a, axis), part)

    def take(source):
        return jax.tree.map(lambda a: lax.dynamic_index_in_dim(a, source, 0, False), gathered)

    return lax.fori_loop(
        1, lax.axis_size(axis), lambda source, state: combine(state, take(source)), take(0)
    )


def apply_rotary(values, token_position):
    half_dim = values.shape[-1] // 2
    inverse = ROPE_BASE ** (-jnp.arange(half_dim, dtype=jnp.float32) * 2.0 / values.shape[-1])
    angles = token_position[..., None] * inverse
    cosine = jnp.concatenate([jnp.cos(angles), jnp.cos(angles)], -1)
    sine_table = jnp.concatenate([jnp.sin(angles), jnp.sin(angles)], -1)
    turned = jnp.concatenate([-values[..., half_dim:], values[..., :half_dim]], -1)
    return values * cosine + turned * sine_table


def combine_pair(former, latter):
    highest = jnp.maximum(former[0], latter[0])
    former_scale = jnp.exp(former[0] - highest)
    latter_scale = jnp.exp(latter[0] - highest)
    return (
        highest,
        former[1] * former_scale + latter[1] * latter_scale,
        former[2] * former_scale[..., None] + latter[2] * latter_scale[..., None],
    )


def per_device(
    hidden,
    input_norm_gain,
    lengths,
    key_value_cache,
    query_base_weight,
    key_value_weight,
    output_weight,
    adapter_down,
    query_up_factor,
    key_value_up,
):
    step_total, row_total, model_width = hidden.shape
    group_width = QUERY_HEADS // KEY_VALUE_HEADS
    tensor_rank = lax.axis_index("tensor")
    local_cols = query_base_weight.shape[1]
    local_heads = local_cols // HEAD_DIM
    widened = hidden.astype(jnp.float32)
    normed = (
        widened
        * lax.rsqrt(jnp.mean(widened * widened, -1, keepdims=True) + NORM_EPSILON)
        * input_norm_gain.astype(jnp.float32)
    ).astype(jnp.bfloat16)
    flattened_rows = normed.reshape(step_total * row_total, model_width)
    query_delta, key_value_delta = (
        lax.all_gather(query_up_factor, "learner", axis=0, tiled=True),
        lax.all_gather(key_value_up, "learner", axis=1, tiled=True),
    )
    adapter_rank = query_delta.shape[0]
    down_slice = lax.all_gather(adapter_down, ("learner", "tensor"), axis=0, tiled=True)
    query_rows = (
        query_base_weight.astype(jnp.float32)
        + ADAPTER_SCALE
        * jnp.dot(down_slice[:, :adapter_rank], query_delta, preferred_element_type=jnp.float32)
    ).astype(jnp.bfloat16)
    key_rows = (
        key_value_weight[0].astype(jnp.float32)
        + ADAPTER_SCALE
        * jnp.dot(
            down_slice[:, adapter_rank : 2 * adapter_rank],
            key_value_delta[0],
            preferred_element_type=jnp.float32,
        )
    ).astype(jnp.bfloat16)
    value_row_list = (
        key_value_weight[1].astype(jnp.float32)
        + ADAPTER_SCALE
        * jnp.dot(
            down_slice[:, 2 * adapter_rank :],
            key_value_delta[1],
            preferred_element_type=jnp.float32,
        )
    ).astype(jnp.bfloat16)
    query_sum = jnp.dot(flattened_rows, query_rows, preferred_element_type=jnp.float32)
    key_sum = jnp.dot(flattened_rows, key_rows, preferred_element_type=jnp.float32)
    value_sum = jnp.dot(flattened_rows, value_row_list, preferred_element_type=jnp.float32)
    merged_query_weight = query_rows
    kv_merged = jnp.stack([key_rows, value_row_list])
    query_sum, key_sum, value_sum, merged_query_weight, kv_merged = (
        query_sum,
        key_sum,
        value_sum,
        merged_query_weight,
        kv_merged,
    )
    token_position = (lengths[None, :] + jnp.arange(step_total, dtype=jnp.int32)[:, None]).astype(
        jnp.float32
    )
    own_query = apply_rotary(
        query_sum.reshape(step_total, row_total, local_heads, HEAD_DIM), token_position[:, :, None]
    ).astype(jnp.bfloat16)
    query_heads_all, key_all, value_heads_all = (
        lax.all_gather(
            own_query.reshape(step_total * row_total, local_cols), "tensor", axis=1, tiled=True
        ),
        lax.all_gather(key_sum.astype(jnp.bfloat16), "tensor", axis=1, tiled=True),
        lax.all_gather(value_sum.astype(jnp.bfloat16), "tensor", axis=1, tiled=True),
    )
    current_keys = apply_rotary(
        lax.optimization_barrier(key_all)
        .astype(jnp.float32)
        .reshape(step_total, row_total, KEY_VALUE_HEADS, HEAD_DIM),
        token_position[:, :, None],
    ).astype(jnp.bfloat16)
    current_values = value_heads_all.reshape(step_total, row_total, KEY_VALUE_HEADS, HEAD_DIM)
    grouped_queries = query_heads_all.reshape(
        step_total, row_total, KEY_VALUE_HEADS, group_width, HEAD_DIM
    )
    block_length = key_value_cache.shape[2]
    stored_keys = key_value_cache[0].reshape(row_total, block_length, KEY_VALUE_HEADS, HEAD_DIM)
    stored_values = key_value_cache[1].reshape(row_total, block_length, KEY_VALUE_HEADS, HEAD_DIM)
    scale_factor = HEAD_DIM ** (-0.5)
    places = tensor_rank * block_length + jnp.arange(block_length, dtype=jnp.int32)
    valid_pos = (places[None, :] < lengths[:, None])[None, :, None, None, :]
    attention_scores = (
        jnp.einsum(
            "srjgd,rpjd->srjgp", grouped_queries, stored_keys, preferred_element_type=jnp.float32
        )
        * scale_factor
    )
    block_max = jnp.max(jnp.where(valid_pos, attention_scores, MASKED_SCORE), -1)
    weights = jnp.where(valid_pos, jnp.exp(attention_scores - block_max[..., None]), 0.0)
    totals = jnp.sum(weights, -1)
    numer_block = jnp.einsum(
        "srjgp,rpjd->srjgd",
        weights.astype(jnp.bfloat16),
        stored_values,
        preferred_element_type=jnp.float32,
    )
    block_max = block_max.reshape(step_total, row_total, QUERY_HEADS)
    totals = totals.reshape(step_total, row_total, QUERY_HEADS)
    numer_block = numer_block.reshape(step_total, row_total, QUERY_HEADS, HEAD_DIM)
    first_head = tensor_rank * local_heads
    full_max, full_total, full_numer = joined(
        (block_max, totals, numer_block), "tensor", combine_pair
    )
    cache_max = lax.dynamic_slice_in_dim(full_max, first_head, local_heads, 2)
    cache_total = lax.dynamic_slice_in_dim(full_total, first_head, local_heads, 2)
    cache_numer = lax.dynamic_slice_in_dim(full_numer, first_head, local_heads, 2)
    own_keys = lax.dynamic_slice_in_dim(
        jnp.repeat(current_keys, group_width, axis=2), first_head, local_heads, 2
    )
    own_values = lax.dynamic_slice_in_dim(
        jnp.repeat(current_values, group_width, axis=2), first_head, local_heads, 2
    )
    fresh = (
        jnp.einsum("srhd,trhd->srht", own_query, own_keys, preferred_element_type=jnp.float32)
        * scale_factor
    )
    causal = (jnp.arange(step_total)[:, None] >= jnp.arange(step_total)[None, :])[:, None, None, :]
    overall = jnp.maximum(cache_max, jnp.max(jnp.where(causal, fresh, MASKED_SCORE), -1))
    cache_weight = jnp.exp(cache_max - overall)
    fresh_weight = jnp.where(causal, jnp.exp(fresh - overall[..., None]), 0.0)
    denominator = cache_total * cache_weight + jnp.sum(fresh_weight, -1)
    numerator = cache_numer * cache_weight[..., None] + jnp.einsum(
        "srht,trhd->srhd", fresh_weight, own_values.astype(jnp.float32)
    )
    attention_result = (
        (numerator / denominator[..., None])
        .astype(jnp.bfloat16)
        .reshape(step_total * row_total, local_cols)
    )
    partial_out = jnp.dot(attention_result, output_weight, preferred_element_type=jnp.float32)
    attended = lax.psum(partial_out, "tensor").astype(jnp.bfloat16)
    return (attended.reshape(step_total, row_total, model_width), merged_query_weight, kv_merged)


def solution(mesh):
    return jax.shard_map(
        per_device,
        mesh=mesh,
        in_specs=(
            P(None, ("groups", "learner"), None),
            P(),
            P(("groups", "learner")),
            P(None, ("groups", "learner"), "tensor", None),
            P(None, "tensor"),
            P(None, None, "tensor"),
            P("tensor", None),
            P(("groups", "learner", "tensor"), None),
            P(("groups", "learner"), "tensor"),
            P(None, ("groups", "learner"), "tensor"),
        ),
        out_specs=(
            P(None, ("groups", "learner"), None),
            P("groups", "tensor"),
            P(None, "groups", "tensor"),
        ),
        check_vma=False,
    )
```

profile of v0, /device:TPU:0, one launch (start us, length us, event | category | flops | bytes accessed | tf_op | source)
XLA Modules:
  0.0 222.1 jit_solution(10073528418169931659)
XLA Ops:
  7.2 0.7 all-gather.6.cloned.1.call-update
  7.9 6.0 %fusion.48 = (bf16[1,8,256,1024]{3,2,1,0:T(8,128)(2,1)}, bf16[1,8,256,1024]{3,2,1,0:T(8,128)(2,1)}) fusion(bf16[2,8,256,1024]{3,2,1,0:T(8,128)(2,1)} %param.15), kind=kLoop, calls=%fused_computation.89 | loop fusion | bytes 16777216 | tf_op jit(solution)/shard_map/slice | solution.py:139
  14.0 6.4 %copy.79 = bf16[1,8,256,1024]{2,3,1,0:T(8,128)(2,1)} copy(bf16[1,8,256,1024]{3,2,1,0:T(8,128)(2,1)} %get-tuple-element.221) | data formatting | bytes 8388608
  20.4 13.7 %copy.49 = bf16[5120,1024]{0,1:T(8,128)(2,1)} copy(bf16[5120,1024]{1,0:T(8,128)(2,1)} %param.16) | data formatting | bytes 20971520 | tf_op args[4]
  34.2 6.5 %copy.80 = bf16[1,8,256,1024]{2,3,1,0:T(8,128)(2,1)} copy(bf16[1,8,256,1024]{3,2,1,0:T(8,128)(2,1)} %get-tuple-element.220) | data formatting | bytes 8388608
  40.7 6.6 %all_gather.33 = bf16[2,64,256]{2,1,0:T(8,128)(2,1)S(1)} all-gather(bf16[2,16,256]{2,1,0:T(8,128)(2,1)S(1)} %copy-done.5), channel_id=1, replica_groups=mesh['groups'=2,'learner'=4,'tensor'=4] {'learner'}, dimensions={1}, use_global_device_ids=true | all-gather | bytes 81920 | tf_op jit(solution)/shard_map/all_gather | solution.py:75
  47.3 5.4 %all_gather.28 = bf16[64,1024]{1,0:T(8,128)(2,1)S(1)} all-gather(bf16[16,1024]{1,0:T(8,128)(2,1)S(1)} %copy-done.4), channel_id=1, replica_groups=mesh['groups'=2,'learner'=4,'tensor'=4] {'learner'}, dimensions={0}, use_global_device_ids=true | all-gather | bytes 163840 | tf_op jit(solution)/shard_map/all_gather | solution.py:74
  52.8 0.1 multiply_cosine_fusion
  53.0 0.1 fusion.17
  53.2 2.1 all-gather.6.cloned.1.call-done
  55.2 4.5 %copy.50 = bf16[16,320,192]{1,0,2:T(8,128)(2,1)} copy(bf16[16,320,192]{1,2,0:T(8,128)(2,1)} %all-gather.6.cloned.1.call-done) | data formatting | bytes 3932160 | tf_op jit(solution)/shard_map/all_gather | solution.py:78
  59.7 4.9 %reshape.156 = bf16[5120,192]{0,1:T(8,128)(2,1)} reshape(bf16[16,320,192]{1,0,2:T(8,128)(2,1)} %copy.50) | data formatting | bytes 3932160
  64.6 3.0 %fusion.5 = bf16[5120,256]{1,0:T(8,128)(2,1)S(1)} fusion(bf16[2,5120,256]{2,1,0:T(8,128)(2,1)} %param.17, bf16[5120,192]{0,1:T(8,128)(2,1)} %reshape.156, bf16[2,64,256]{2,1,0:T(8,128)(2,1)S(1)} %all_gather.33), kind=kOutput, calls=%fused_computation.13 | convolution fusion | flops 173015040 | bytes 5931008 | tf_op jit(solution)/shard_map/dot_general | solution.py:87
  67.6 5.3 %fusion.6 = bf16[5120,256]{1,0:T(8,128)(2,1)} fusion(bf16[2,5120,256]{2,1,0:T(8,128)(2,1)} %param.17, bf16[5120,192]{0,1:T(8,128)(2,1)} %reshape.156, bf16[2,64,256]{2,1,0:T(8,128)(2,1)S(1)} %all_gather.33), kind=kOutput, calls=%fused_computation.14 | convolution fusion | flops 173015040 | bytes 5931008 | tf_op jit(solution)/shard_map/dot_general | solution.py:96
  72.9 0.5 convolution_convert_fusion.1
  73.4 13.1 %all_gather.34 = bf16[16,1024]{1,0:T(8,128)(2,1)S(1)} all-gather(bf16[16,256]{1,0:T(8,128)(2,1)S(1)} %convolution_convert_fusion.1), channel_id=1, replica_groups=mesh['groups'=2,'learner'=4,'tensor'=4] {'tensor'}, dimensions={1}, use_global_device_ids=true | all-gather | bytes 40960 | tf_op jit(solution)/shard_map/all_gather | solution.py:124
  86.6 0.1 slice_negate_fusion
  86.7 6.6 %add_convert_fusion = bf16[5120,1024]{0,1:T(8,128)(2,1)} fusion(bf16[5120,1024]{0,1:T(8,128)(2,1)S(1)} %bitcast.116, bf16[64,1024]{1,0:T(8,128)(2,1)S(1)} %all_gather.28, bf16[5120,192]{0,1:T(8,128)(2,1)} %reshape.156), kind=kOutput, calls=%fused_computation.8 | convolution fusion | flops 692060160 | bytes 21757952 | tf_op jit(solution)/shard_map/dot_general | solution.py:82
  93.3 14.4 %copy.70 = bf16[5120,1024]{1,0:T(8,128)(2,1)} copy(bf16[5120,1024]{0,1:T(8,128)(2,1)} %add_convert_fusion) | data formatting | bytes 20971520
  107.7 5.5 %fusion.24 = f32[2,8,8,128]{3,1,2,0:T(8,128)S(1)} fusion(bf16[8,128,5120,1]{2,1,0,3:T(8,128)(2,1)} %bitcast.114, bf16[2,8,5120]{2,1,0:T(8,128)(2,1)S(1)} %copy-done.3, f32[5120]{0:T(1024)S(1)} %convert_element_type.64, f32[2,8]{1,0:T(2,128)S(1)} %add_rsqrt_fusion), kind=kOutput, calls=%fused_computation.43 | convolution fusion | flops 168099840 | bytes 10735680 | tf_op jit(solution)/shard_map/dot_general | solution.py:102
  113.2 0.1 slice_negate_fusion.1
  113.3 0.1 fusion.32
  113.5 13.5 %all_gather.29 = bf16[16,4096]{1,0:T(8,128)(2,1)S(1)} all-gather(bf16[16,1024]{1,0:T(8,128)(2,1)S(1)} %bitcast.124), channel_id=1, replica_groups=mesh['groups'=2,'learner'=4,'tensor'=4] {'tensor'}, dimensions={1}, use_global_device_ids=true | all-gather | bytes 163840 | tf_op jit(solution)/shard_map/all_gather | solution.py:121
  127.1 3.0 %select_reduce_fusion = (f32[2,8,8,4]{3,0,2,1:T(2,128)S(1)}, f32[2,8,8,4,256]{4,3,0,2,1:T(4,128)S(1)}) fusion(pred[8,256]{1,0:T(8,128)(4,1)S(1)} %broadcast_compare_fusion, bf16[8,256,8,128,1]{1,3,4,2,0:T(8,128)(2,1)} %bitcast.117, bf16[2,8,8,4,128]{4,3,2,1,0:T(4,128)(2,1)S(1)} %reshape.142), kind=kOutput, calls=%fused_computation.31 | convolution fusion | flops 33947136 | bytes 4853760 | tf_op jit(solution)/shard_map/srjgd,rpjd->srjgp/dot_general | solution.py:144
  130.1 0.2 copy.54
  130.3 0.5 fusion.16
  130.8 0.2 copy.56
  131.0 3.6 %convolution_bitcast_fusion = f32[2,8,8,4,128]{4,3,0,2,1:T(4,128)S(1)} fusion(bf16[8,256,8,128,1]{1,3,4,2,0:T(8,128)(2,1)} %bitcast.120, f32[2,8,8,4,256]{4,3,0,2,1:T(4,128)S(1)} %get-tuple-element.231, f32[2,8,8,4]{3,0,2,1:T(2,128)S(1)} %get-tuple-element.230, pred[8,256]{1,0:T(8,128)(4,1)S(1)} %broadcast_compare_fusion), kind=kOutput, calls=%fused_computation.18 | convolution fusion | flops 33947648 | bytes 4984832 | tf_op jit(solution)/shard_map/srjgp,rpjd->srjgd/dot_general | solution.py:152
  134.6 0.2 copy.60
  134.8 0.8 copy.61
  135.7 2.4 %convolution_convert_fusion = bf16[16,256]{1,0:T(8,128)(2,1)S(1)} fusion(bf16[5120,256]{1,0:T(8,128)(2,1)} %fusion.6, bf16[2,8,5120]{2,1,0:T(8,128)(2,1)S(1)} %copy-done.3, f32[5120]{0:T(1024)S(1)} %convert_element_type.64, f32[2,8]{1,0:T(2,128)S(1)} %add_rsqrt_fusion), kind=kOutput, calls=%fused_computation.25 | convolution fusion | flops 42274816 | bytes 2814016 | tf_op jit(solution)/shard_map/dot_general | solution.py:104
  138.0 13.2 %all_gather.35 = bf16[16,1024]{1,0:T(8,128)(2,1)S(1)} all-gather(bf16[16,256]{1,0:T(8,128)(2,1)S(1)} %convolution_convert_fusion), channel_id=1, replica_groups=mesh['groups'=2,'learner'=4,'tensor'=4] {'tensor'}, dimensions={1}, use_global_device_ids=true | all-gather | bytes 40960 | tf_op jit(solution)/shard_map/all_gather | solution.py:125
  151.3 13.2 %all_gather.30 = f32[4,2,8,32]{3,2,1,0:T(8,128)S(1)} all-gather(f32[1,2,8,32]{3,2,1,0:T(8,128)S(1)} %copy.55), channel_id=1, replica_groups=mesh['groups'=2,'learner'=4,'tensor'=4] {'tensor'}, dimensions={0}, use_global_device_ids=true | all-gather | bytes 10240 | tf_op jit(solution)/shard_map/all_gather | solution.py:18
  164.5 13.1 %all_gather.31 = f32[4,2,8,32]{3,2,1,0:T(8,128)S(1)} all-gather(f32[1,2,8,32]{3,2,1,0:T(8,128)S(1)} %copy.57), channel_id=1, replica_groups=mesh['groups'=2,'learner'=4,'tensor'=4] {'tensor'}, dimensions={0}, use_global_device_ids=true | all-gather | bytes 10240 | tf_op jit(solution)/shard_map/all_gather | solution.py:18
  177.7 0.3 select_reduce_fusion.1
  178.0 2.8 %pad_maximum_fusion = bf16[2,5120,256]{2,1,0:T(8,128)(2,1)} fusion(bf16[1,5120,256]{2,1,0:T(8,128)(2,1)S(1)} %bitcast.119, bf16[1,5120,256]{2,1,0:T(8,128)(2,1)S(1)} %bitcast.118), kind=kLoop, calls=%fused_computation.15 | loop fusion | flops 2621440 | bytes 10485760 | tf_op jit(solution)/shard_map/stack | solution.py:106
  180.8 1.0 slice_bitcast_fusion
  181.8 3.8 %while.19 = (s32[]{:T(128)}, f32[2,8,32]{2,1,0:T(8,128)S(1)}, f32[2,8,32]{2,1,0:T(8,128)S(1)}, f32[2,8,32,128]{3,2,1,0:T(8,128)S(1)}, f32[4,2,8,32]{3,2,1,0:T(8,...) while((s32[]{:T(128)}, f32[2,8,32]{2,1,0:T(8,128)S(1)}, ...), condition=%wide.region_4.5_spmd, body=%wide.region_3.4_spmd.sunk | while | flops 199685 | bytes 807063 | solution.py:23
  181.8 1.2 fusion.59
  183.1 1.2 fusion.59
  184.3 1.2 fusion.59
  185.6 0.2 copy.62
  185.8 0.1 copy.63
  185.9 0.1 copy.68
  186.1 0.1 fusion.42
  186.3 0.3 fusion.11
  186.6 5.5 %fusion.36 = f32[16,5120]{1,0:T(8,128)S(1)} fusion(bf16[1024,5120]{1,0:T(8,128)(2,1)} %param.18, bf16[2,8,8,128]{3,2,1,0:T(8,128)(2,1)S(1)} %copy.95), kind=kOutput, calls=%fused_computation.59 | convolution fusion | flops 167772160 | bytes 10846208 | tf_op jit(solution)/shard_map/dot_general | solution.py:191
  192.1 23.2 %all-reduce.1 = bf16[16,5120]{1,0:T(8,128)(2,1)} all-reduce(f32[16,5120]{1,0:T(8,128)S(1)} %fusion.36), channel_id=1, replica_groups=mesh['groups'=2,'learner'=4,'tensor'=4] {'tensor'}, use_global_device_ids=true, to_apply=%region_7.8 | all-reduce | flops 81920 | bytes 491520 | tf_op jit(solution)/shard_map/psum | solution.py:192
  (51 shorter events, 0.9 us)
Async XLA Ops:
  7.2 48.1 %all-gather.6.cloned.1.call-start = ((), (), s32[]{:S(2)}) async-start(), calls=%async_computation.1 | async-start | bytes 2506752 | tf_op jit(solution)/shard_map/all_gather | solution.py:78
  7.9 172.9 %all-gather.4.cloned.1.call-start = ((), (), s32[]{:S(2)}) async-start(), calls=%async_computation | async-start | bytes 1310720 | tf_op jit(solution)/shard_map/all_gather | solution.py:18
  14.0 6.4 %copy-start.6 = (bf16[5120]{0:T(1024)(128)(2,1)S(1)}, bf16[5120]{0:T(1024)(128)(2,1)}, u32[]{:S(2)}) copy-start(bf16[5120]{0:T(1024)(128)(2,1)} %param.13) | copy-start | bytes 30724
  34.1 6.6 %copy-start.5 = (bf16[2,16,256]{2,1,0:T(8,128)(2,1)S(1)}, bf16[2,16,256]{2,1,0:T(8,128)(2,1)}, u32[]{:S(2)}) copy-start(bf16[2,16,256]{2,1,0:T(8,128)(2,1)} %param.21) | copy-start | bytes 49156
  34.1 13.2 %copy-start.4 = (bf16[16,1024]{1,0:T(8,128)(2,1)S(1)}, bf16[16,1024]{1,0:T(8,128)(2,1)}, u32[]{:S(2)}) copy-start(bf16[16,1024]{1,0:T(8,128)(2,1)} %param.20) | copy-start | bytes 98308
  34.1 18.6 %copy-start.7 = (s32[8]{0:T(128)S(1)}, s32[8]{0:T(128)}, u32[]{:S(2)}) copy-start(s32[8]{0:T(128)} %param.14) | copy-start | bytes 100
  34.1 18.8 %copy-start.3 = (bf16[2,8,5120]{2,1,0:T(8,128)(2,1)S(1)}, bf16[2,8,5120]{2,1,0:T(8,128)(2,1)}, u32[]{:S(2)}) copy-start(bf16[2,8,5120]{2,1,0:T(8,128)(2,1)} %param.12) | copy-start | bytes 491524
  59.7 26.9 %slice-start = ((s8[10485760]{0:T(1024)(128)(4,1)}), s8[2097152]{0:T(1024)(128)(4,1)S(1)}, s32[]{:S(2)}) async-start(s8[10485760]{0:T(1024)(128)(4,1)} %bitcast.115), calls=%async_computation.2 | async-start | bytes 4194304
  64.6 22.0 %slice-start.1 = ((s8[10485760]{0:T(1024)(128)(4,1)}), s8[4194304]{0:T(1024)(128)(4,1)S(1)}, s32[]{:S(2)}) async-start(s8[10485760]{0:T(1024)(128)(4,1)} %bitcast.115), calls=%async_computation.3 | async-start | bytes 8388608
  67.6 5.3 %copy-start = (bf16[5120,256]{1,0:T(8,128)(2,1)}, bf16[5120,256]{1,0:T(8,128)(2,1)S(1)}, u32[]{:S(2)}) copy-start(bf16[5120,256]{1,0:T(8,128)(2,1)S(1)} %fusion.5) | copy-start | bytes 7864324
  67.6 19.1 %slice-start.2 = ((s8[10485760]{0:T(1024)(128)(4,1)}), s8[4194304]{0:T(1024)(128)(4,1)S(1)}, s32[]{:S(2)}) async-start(s8[10485760]{0:T(1024)(128)(4,1)} %bitcast.115), calls=%async_computation.4 | async-start | bytes 8388608
  131.0 46.9 %copy-start.1 = (bf16[5120,256]{1,0:T(8,128)(2,1)S(1)}, bf16[5120,256]{1,0:T(8,128)(2,1)}, u32[]{:S(2)}) copy-start(bf16[5120,256]{1,0:T(8,128)(2,1)} %copy-done) | copy-start | bytes 7864324
  135.6 42.4 %copy-start.2 = (bf16[5120,256]{1,0:T(8,128)(2,1)S(1)}, bf16[5120,256]{1,0:T(8,128)(2,1)}, u32[]{:S(2)}) copy-start(bf16[5120,256]{1,0:T(8,128)(2,1)} %fusion.6) | copy-start | bytes 7864324
Sparse Core Ops, SparseCore 0:
  10.3 44.8 all-gather.5
  135.7 28.0 all-gather.3
where the time goes:
time: 224 us; the launch traced here: 222 us
  blocking collectives  101 us (45%)
  local copies, waits for them, and re-layouts  59.7 us (27%)
  matrix products  35.9 us (16%)
  between operations  14.3 us (6%)
  other arithmetic  7.87 us (4%)
  waiting for transfers between devices  2.76 us (1%)
    unnamed x27, local copies, waits for them, and re-layouts  46.1 us
    all_gather x2, blocking collectives, joined(): gathered = jax.tree.map(lambda a: lax.all_gather(a, axis), part)  26.3 us
    psum x1, blocking collectives, per_device(): attended = lax.psum(partial_out, 'tensor').astype(jnp.bfloat16)  23.2 us
    all_gather x1, blocking collectives, per_device(): lax.all_gather(own_query.reshape(step_total * row_total, local_cols), 'te...  13.5 us
    all_gather x1, blocking collectives, per_device(): lax.all_gather(value_sum.astype(jnp.bfloat16), 'tensor', axis=1, tiled=True)  13.2 us
    all_gather x1, blocking collectives, per_device(): lax.all_gather(key_sum.astype(jnp.bfloat16), 'tensor', axis=1, tiled=True)  13.1 us
    dot_general x1, matrix products, per_device(): jnp.dot(down_slice[:, :adapter_rank], query_delta, preferred_element_type...  6.65 us
    all_gather x1, blocking collectives, per_device(): lax.all_gather(key_value_up, 'learner', axis=1, tiled=True)  6.61 us
  transfers between devices with their start and end apart: 2, of which 1 were waited for; matrix products, arithmetic and copies ran while one was open for 17% of the time, Pallas kernels for 0%

commit v1 on v0

--- a/solution.py
+++ b/solution.py
@@ -1,11 +1,15 @@
+import math
 import jax
 import jax.numpy as jnp
 from jax import lax
+from jax.experimental import pallas as pl
+from jax.experimental.pallas import tpu as pltpu
 from jax.sharding import PartitionSpec as P
 
 QUERY_HEADS = 32
 KEY_VALUE_HEADS = 8
 HEAD_DIM = 128
+MESH = pl.DeviceIdType.MESH
 
 
 ADAPTER_SCALE = 2.0
@@ -193,9 +197,391 @@
     return (attended.reshape(step_total, row_total, model_width), merged_query_weight, kv_merged)
 
 
+def gather_kernel(
+    hidden_ref, gain_ref, down_ref, upq_ref, upkv_ref,
+    pall_ref, uq_ref, uk_ref, uv_ref, nb_ref,
+    pk, upq_g, upkv_g, up_send, up_recv, b_send, b_recv, own_sem,
+):
+    f32, bf16 = jnp.float32, jnp.bfloat16
+    L, T = 4, 4
+    l, t = lax.axis_index("learner"), lax.axis_index("tensor")
+    tp = [lax.rem(t + d, T) for d in range(T)]
+    lp = [lax.rem(l + d, L) for d in range(L)]
+    barrier = pltpu.get_barrier_semaphore()
+    for d in range(1, 4):
+        pl.semaphore_signal(barrier, inc=1, device_id={"tensor": tp[d]}, device_id_type=MESH)
+        pl.semaphore_signal(barrier, inc=1, device_id={"learner": lp[d]}, device_id_type=MESH)
+    shard = down_ref[...]
+    rows = shard.shape[0]
+    half = rows // 2
+    pk[0:rows, :] = shard[:, :128]
+    pk[rows : rows + half, :] = jnp.concatenate([shard[:half, 128:], shard[half:, 128:]], axis=1)
+    pl.semaphore_wait(barrier, 6)
+
+    waits = []
+    l2 = lax.rem(l + 2, L)
+    l1 = l + 1 - 2 * lax.rem(l, 2)
+    l3 = lax.rem(l1 + 2, L)
+    t1 = t + 1 - 2 * lax.rem(t, 2)
+    zp = [t, t1, lax.rem(t + 2, T), lax.rem(t1 + 2, T)]
+
+    def bulk(src, blk, dev):
+        c = pltpu.make_async_remote_copy(
+            src_ref=src, dst_ref=pall_ref.at[blk], send_sem=b_send.at[len(waits)], recv_sem=b_recv.at[blk],
+            device_id=dev, device_id_type=MESH,
+        )
+        c.start()
+        waits.append(c)
+
+    def arrived(blk):
+        pltpu.make_async_remote_copy(
+            src_ref=pk, dst_ref=pall_ref.at[blk], send_sem=b_send.at[0], recv_sem=b_recv.at[blk],
+            device_id={"tensor": t1}, device_id_type=MESH,
+        ).wait_recv()
+
+    b = l * T + t
+    bulk(pk, b, {"learner": l2})
+    for k in (1, 2, 3):
+        bulk(pk, b, {"tensor": zp[k]})
+    bulk(pk, b, {"learner": l1})
+    own = pltpu.make_async_copy(pk, pall_ref.at[b], own_sem)
+    own.start()
+    ups = []
+    for d in range(1, 4):
+        for k, (src, dst) in enumerate(((upq_ref, upq_g), (upkv_ref, upkv_g))):
+            c = pltpu.make_async_remote_copy(
+                src_ref=src, dst_ref=dst.at[l], send_sem=up_send.at[k, d], recv_sem=up_recv.at[k, d],
+                device_id={"learner": lp[d]}, device_id_type=MESH,
+            )
+            c.start()
+            ups.append(c)
+    upq_g[l] = upq_ref[...]
+    upkv_g[l] = upkv_ref[...]
+
+    model = gain_ref.shape[1]
+    wide = hidden_ref[...].astype(f32).reshape(16, model)
+    inv = lax.rsqrt(jnp.mean(wide * wide, -1, keepdims=True) + NORM_EPSILON)
+    normed = (wide * inv * gain_ref[...].astype(f32)).astype(bf16)
+    wid = nb_ref.shape[2]
+    for k in range(nb_ref.shape[0]):
+        nb_ref[k] = normed[:, k * wid : (k + 1) * wid]
+    uq_ref[...] = jnp.zeros_like(uq_ref)
+    uk_ref[...] = jnp.zeros_like(uk_ref)
+    uv_ref[...] = jnp.zeros_like(uv_ref)
+
+    for k in (1, 2, 3):
+        blk = l * T + zp[k]
+        arrived(blk)
+        bulk(pall_ref.at[blk], blk, {"learner": l2})
+        bulk(pall_ref.at[blk], blk, {"learner": l1})
+        blk = l2 * T + zp[k - 1]
+        arrived(blk)
+        bulk(pall_ref.at[blk], blk, {"learner": l1})
+    for c in ups:
+        c.wait_recv()
+    uq_ref[0:64, :] = upq_g[...].reshape(64, upq_g.shape[2])
+    kvg = upkv_g[...]
+    uk_ref[64:128, :] = kvg[:, 0].reshape(64, upkv_g.shape[3])
+    uv_ref[64:128, :] = kvg[:, 1].reshape(64, upkv_g.shape[3])
+    blk = l2 * T + zp[3]
+    arrived(blk)
+    bulk(pall_ref.at[blk], blk, {"learner": l1})
+    for k in range(4):
+        arrived(l1 * T + k)
+        arrived(l3 * T + k)
+    own.wait()
+    for c in ups + waits:
+        c.wait_send()
+
+
+def merge_kernel(
+    p_ref, uq_ref, uk_ref, uv_ref, n_ref, wq_ref, wkv_ref, oq_ref, okv_ref, qs_ref, ks_ref, vs_ref
+):
+    f32, bf16 = jnp.float32, jnp.bfloat16
+    rows = p_ref.shape[1] * 2 // 3
+    half = rows // 2
+
+    @pl.when(pl.program_id(0) == 0)
+    def _():
+        qs_ref[...] = jnp.zeros_like(qs_ref)
+        ks_ref[...] = jnp.zeros_like(ks_ref)
+        vs_ref[...] = jnp.zeros_like(vs_ref)
+
+    uv_high = uv_ref[...]
+    uv_low = jnp.concatenate([uv_high[64:], uv_high[:64]], axis=0)
+    for e in range(p_ref.shape[0]):
+        p = p_ref[e]
+        qk, pv = p[:rows], p[rows:]
+        cut = slice(e * rows, (e + 1) * rows)
+        dq = jnp.dot(qk, uq_ref[...], preferred_element_type=f32)
+        oq_ref[cut] = (wq_ref[cut].astype(f32) + ADAPTER_SCALE * dq).astype(bf16)
+        dk = jnp.dot(qk, uk_ref[...], preferred_element_type=f32)
+        okv_ref[0, cut] = (wkv_ref[0, cut].astype(f32) + ADAPTER_SCALE * dk).astype(bf16)
+        for k, up in enumerate((uv_low, uv_high)):
+            dv = jnp.dot(pv, up, preferred_element_type=f32)
+            cut = slice(e * rows + k * half, e * rows + (k + 1) * half)
+            okv_ref[1, cut] = (wkv_ref[1, cut].astype(f32) + ADAPTER_SCALE * dv).astype(bf16)
+    n = n_ref[0]
+    qs_ref[...] += jnp.dot(n, oq_ref[...], preferred_element_type=f32)
+    ks_ref[...] += jnp.dot(n, okv_ref[0], preferred_element_type=f32)
+    vs_ref[...] += jnp.dot(n, okv_ref[1], preferred_element_type=f32)
+
+
+def decode_kernel(
+    lengths_ref, qs_ref, ks_ref, vs_ref, cache_hbm, wo_hbm,
+    att_ref,
+    kc, vc, wo,
+    qtmp, qall, keyf, valf, nsend, nrecv, msend, mrecv, res, abuf,
+    psend, precv, asend, arecv,
+    load_sem, q_send, q_recv, n_send, n_recv, m_send, m_recv, p_send, p_recv, a_send, a_recv,
+):
+    f32, bf16 = jnp.float32, jnp.bfloat16
+    T = 4
+    t = lax.axis_index("tensor")
+    model = wo.shape[1]
+    scale = HEAD_DIM ** (-0.5)
+    tp = [lax.rem(t + d, T) for d in range(T)]
+
+    def to_t(d):
+        return {"tensor": tp[d]}
+
+    barrier = pltpu.get_barrier_semaphore()
+    for d in range(1, 4):
+        pl.semaphore_signal(barrier, inc=1, device_id=to_t(d), device_id_type=MESH)
+    loads = [
+        pltpu.make_async_copy(cache_hbm.at[0], kc, load_sem.at[0]),
+        pltpu.make_async_copy(cache_hbm.at[1], vc, load_sem.at[1]),
+        pltpu.make_async_copy(wo_hbm, wo, load_sem.at[2]),
+    ]
+    for c in loads:
+        c.start()
+    waits = []
+
+    def send(src, dst, ssem, rsem, dev):
+        c = pltpu.make_async_remote_copy(
+            src_ref=src, dst_ref=dst, send_sem=ssem, recv_sem=rsem, device_id=dev, device_id_type=MESH
+        )
+        c.start()
+        waits.append(c)
+        return c
+
+    sub = lax.broadcasted_iota(jnp.int32, (16, 128), 0)
+    lane = lax.broadcasted_iota(jnp.int32, (16, 128), 1)
+    row = lax.rem(sub, 8)
+    pos = jnp.zeros((16, 128), jnp.int32)
+    for r in range(8):
+        pos = jnp.where(row == r, lengths_ref[r], pos)
+    pos = (pos + jnp.where(sub >= 8, 1, 0)).astype(f32)
+    freq = jnp.exp(lax.rem(lane, 64).astype(f32) * (-2.0 / HEAD_DIM * math.log(ROPE_BASE)))
+    cosine = jnp.cos(pos * freq)
+    sine = jnp.sin(pos * freq)
+    sine = jnp.where(lane < 64, -sine, sine)
+
+    def rope(v):
+        return v * cosine + pltpu.roll(v, 64, 1) * sine
+
+    qacc = qs_ref[...]
+    kacc = ks_ref[...].astype(bf16).astype(f32)
+    valf[...] = vs_ref[...].astype(bf16).astype(f32)
+    pl.semaphore_wait(barrier, 3)
+
+    for h in range(8):
+        v = rope(qacc[:, h * 128 : (h + 1) * 128])
+        for s in range(2):
+            start = (h // 4) * 8 + s * 4 + h % 4
+            qtmp[pl.ds(start, 8, stride=16), :] = v[s * 8 : (s + 1) * 8, :]
+    qall[0] = qtmp[...].astype(bf16)
+    qs = [send(qall.at[0], qall.at[d], q_send.at[d], q_recv.at[d], to_t(d)) for d in range(1, 4)]
+    for h in range(2):
+        keyf[:, h * 128 : (h + 1) * 128] = rope(kacc[:, h * 128 : (h + 1) * 128]).astype(bf16).astype(f32)
+
+    loads[0].wait()
+    loads[1].wait()
+    first = sub[:, 0:1] < 8
+    place = t * kc.shape[1] + lax.broadcasted_iota(jnp.int32, (16, kc.shape[1]), 1)
+    lane2 = lane
+    ns_copies = [None] * 4
+    per = 4
+
+    def attend(d):
+        owner = lax.rem(t + T - d, T)
+        cols = pl.multiple_of(owner * 256, 256)
+
+        def step(i, ml):
+            for u in range(per):
+                r = i * per + u
+                q16 = qall[d, pl.ds(pl.multiple_of(r * 16, 16), 16), :]
+                kk = kc[r, :, pl.ds(cols, 256)]
+                vv = vc[r, :, pl.ds(cols, 256)]
+                dims = (((1,), (1,)), ((), ()))
+                s0 = lax.dot_general(q16, kk[:, :128], dims, preferred_element_type=f32)
+                s1 = lax.dot_general(q16, kk[:, 128:], dims, preferred_element_type=f32)
+                s = jnp.where(first, s0, s1) * scale
+                valid = place < lengths_ref[r]
+                m = jnp.max(jnp.where(valid, s, MASKED_SCORE), -1, keepdims=True)
+                w = jnp.where(valid, jnp.exp(s - m), 0.0)
+                tot = jnp.sum(w, -1, keepdims=True)
+                nn = jnp.dot(w.astype(bf16), vv, preferred_element_type=f32)
+                nn = jnp.where(first, nn[:, :128], nn[:, 128:])
+                nsend[d, pl.ds(pl.multiple_of(r * 16, 16), 16), :] = nn.astype(nsend.dtype)
+                ml = jnp.where(lane2 == r, m, jnp.where(lane2 == r + 8, tot, ml))
+            return ml
+
+        msend[d] = lax.fori_loop(0, 8 // per, step, jnp.zeros((16, 128), f32))
+
+    attend(0)
+    nsc, msc = [], []
+    for d in range(1, 4):
+        qs[d - 1].wait_recv()
+        attend(d)
+        back = 4 - d
+        nsc.append(send(nsend.at[d], nrecv.at[back], n_send.at[d], n_recv.at[back], to_t(back)))
+        msc.append(send(msend.at[d], mrecv.at[back], m_send.at[d], m_recv.at[back], to_t(back)))
+
+    for c in nsc:
+        c.wait_recv()
+    for c in msc:
+        c.wait_recv()
+    nrecv[0] = nsend[0]
+    mrecv[0] = msend[0]
+    late = lax.rem(sub[:, 0:1] // 4, 2) == 1
+    for r in range(8):
+        q16 = qall[0, r * 16 : (r + 1) * 16, :].astype(f32)
+        fresh = []
+        vals = []
+        for u in range(2):
+            k16 = jnp.where(first, keyf[u * 8 + r : u * 8 + r + 1, 0:128], keyf[u * 8 + r : u * 8 + r + 1, 128:256])
+            vals.append(
+                jnp.where(first, valf[u * 8 + r : u * 8 + r + 1, 0:128], valf[u * 8 + r : u * 8 + r + 1, 128:256])
+            )
+            fresh.append(jnp.sum(q16 * k16, -1, keepdims=True) * scale)
+        fresh[1] = jnp.where(late, fresh[1], MASKED_SCORE)
+        ms = [mrecv[d, :, r : r + 1] for d in range(4)]
+        top = jnp.maximum(fresh[0], fresh[1])
+        for m in ms:
+            top = jnp.maximum(top, m)
+        w0 = jnp.exp(fresh[0] - top)
+        w1 = jnp.where(late, jnp.exp(fresh[1] - top), 0.0)
+        den = w0 + w1
+        num = w0 * vals[0] + w1 * vals[1]
+        for d in range(4):
+            e = jnp.exp(ms[d] - top)
+            den = den + e * mrecv[d, :, 8 + r : 9 + r]
+            num = num + e * nrecv[d, r * 16 : (r + 1) * 16, :].astype(f32)
+        res[r * 16 : (r + 1) * 16, :] = num / den
+    for h in range(8):
+        for s in range(2):
+            start = (h // 4) * 8 + s * 4 + h % 4
+            abuf[s * 8 : (s + 1) * 8, h * 128 : (h + 1) * 128] = res[pl.ds(start, 8, stride=16), :]
+    a = abuf[...].astype(bf16)
+
+    loads[2].wait()
+    quarter = model // T
+    ps = []
+    for d in (2, 1, 3):
+        o = jnp.dot(a, wo[:, pl.ds(pl.multiple_of(tp[d] * quarter, 128), quarter)], preferred_element_type=f32)
+        psend[d] = o.astype(bf16)
+        ps.append(send(psend.at[d], precv.at[d], p_send.at[d], p_recv.at[d], to_t(d)))
+    total = jnp.dot(a, wo[:, pl.ds(pl.multiple_of(t * quarter, 128), quarter)], preferred_element_type=f32)
+
+    for c in ps:
+        c.wait_recv()
+    for d in range(1, 4):
+        total = total + precv[d].astype(f32)
+    asend[...] = total.astype(bf16)
+    acs = [send(asend, arecv.at[t], a_send.at[d], a_recv.at[d], to_t(d)) for d in range(1, 4)]
+    arecv[t] = asend[...]
+    for c in acs:
+        c.wait_recv()
+    for k in range(4):
+        both = arecv[k].astype(f32)
+        for s in range(2):
+            att_ref[s, :, k * quarter : (k + 1) * quarter] = both[s * 8 : (s + 1) * 8, :].astype(bf16)
+    for c in waits:
+        c.wait_send()
+
+
+def fused_device(
+    hidden, input_norm_gain, lengths, key_value_cache, query_base_weight, key_value_weight,
+    output_weight, adapter_down, query_up_factor, key_value_up,
+):
+    f32, bf16 = jnp.float32, jnp.bfloat16
+    model = hidden.shape[2]
+    part = model // 4
+    rows = adapter_down.shape[0]
+    packed = rows + rows // 2
+    steps = 8
+    V, A, S = pltpu.VMEM, pl.ANY, pltpu.SMEM
+    dma = pltpu.SemaphoreType.DMA
+    spec = lambda m: pl.BlockSpec(memory_space=m)
+    shape = jax.ShapeDtypeStruct
+    p_all, uq, uk, uv, blocks = pl.pallas_call(
+        gather_kernel,
+        out_shape=[
+            shape((16, packed, 128), bf16), shape((128, 1024), bf16), shape((128, 256), bf16),
+            shape((128, 256), bf16), shape((steps, 16, model // steps), bf16),
+        ],
+        in_specs=[spec(V)] * 5,
+        out_specs=[spec(A)] + [spec(V)] * 4,
+        scratch_shapes=[
+            V((packed, 128), bf16), V((4, 16, 1024), bf16), V((4, 2, 16, 256), bf16),
+            dma((2, 4)), dma((2, 4)), dma((15,)), dma((16,)), dma,
+        ],
+        compiler_params=pltpu.CompilerParams(
+            collective_id=0, has_side_effects=True, vmem_limit_bytes=32 * 1024 * 1024
+        ),
+        name="gather",
+    )(hidden, input_norm_gain.reshape(1, model), adapter_down, query_up_factor, key_value_up)
+    wide = model // steps
+    whole = lambda *sh: pl.BlockSpec(sh, lambda i: (0,) * len(sh))
+    merged, kv_merged, qs, ks, vs = pl.pallas_call(
+        merge_kernel,
+        grid=(steps,),
+        out_shape=[
+            shape(query_base_weight.shape, bf16), shape(key_value_weight.shape, bf16),
+            shape((16, 1024), f32), shape((16, 256), f32), shape((16, 256), f32),
+        ],
+        in_specs=[
+            pl.BlockSpec((16 // steps, packed, 128), lambda i: (i, 0, 0)),
+            whole(128, 1024), whole(128, 256), whole(128, 256),
+            pl.BlockSpec((1, 16, wide), lambda i: (i, 0, 0)),
+            pl.BlockSpec((wide, 1024), lambda i: (i, 0)),
+            pl.BlockSpec((2, wide, 256), lambda i: (0, i, 0)),
+        ],
+        out_specs=[
+            pl.BlockSpec((wide, 1024), lambda i: (i, 0)),
+            pl.BlockSpec((2, wide, 256), lambda i: (0, i, 0)),
+            whole(16, 1024), whole(16, 256), whole(16, 256),
+        ],
+        compiler_params=pltpu.CompilerParams(vmem_limit_bytes=40 * 1024 * 1024),
+        name="merge",
+    )(p_all, uq, uk, uv, blocks, query_base_weight, key_value_weight)
+    attended = pl.pallas_call(
+        decode_kernel,
+        out_shape=shape(hidden.shape, bf16),
+        in_specs=[spec(S)] + [spec(V)] * 3 + [spec(A)] * 2,
+        out_specs=spec(V),
+        scratch_shapes=[
+            V((8, 256, 1024), bf16), V((8, 256, 1024), bf16), V((1024, model), bf16),
+            V((128, 128), f32), V((4, 128, 128), bf16), V((16, 256), f32), V((16, 256), f32),
+            V((4, 128, 128), bf16), V((4, 128, 128), bf16), V((4, 16, 128), f32), V((4, 16, 128), f32),
+            V((128, 128), f32), V((16, 1024), f32),
+            V((4, 16, part), bf16), V((4, 16, part), bf16), V((16, part), bf16), V((4, 16, part), bf16),
+            dma((3,)),
+        ]
+        + [dma((4,))] * 10,
+        compiler_params=pltpu.CompilerParams(
+            collective_id=1, has_side_effects=True, vmem_limit_bytes=48 * 1024 * 1024
+        ),
+        name="decode",
+    )(lengths, qs, ks, vs, key_value_cache, output_weight)
+    return attended, merged, kv_merged
+
+
 def solution(mesh):
+    small = mesh.shape["learner"] == 4 and mesh.shape["tensor"] == 4
     return jax.shard_map(
-        per_device,
+        fused_device if small else per_device,
         mesh=mesh,
         in_specs=(
             P(None, ("groups", "learner"), None),

time: 224 us -> 73.1 us (0.33)
  blocking collectives: 101 us -> 0 us
  Pallas kernels: 0 us -> 64.6 us
  local copies, waits for them, and re-layouts: 59.7 us -> 7.28 us
  matrix products: 35.9 us -> 0 us
  between operations: 14.3 us -> 0.68 us
  other arithmetic: 7.87 us -> 0 us
  waiting for transfers between devices: 2.76 us -> 0 us
    all_gather x7 -> x0, blocking collectives: 78.2 us -> none  [the longest x2 26.3 us: joined(): gathered = jax.tree.map(lambda a: lax.all_gather(a, axis), part)]
    pallas_call x0 -> x3, Pallas kernels: none -> 64.6 us  [the longest x1 28.5 us: fused_device(): pl.pallas_call(decode_kernel, out_shape=shape(hidden.shape, bf16), in_spe...]
    unnamed x27 -> x12, local copies, waits for them, and re-layouts: 46.1 us -> 6.57 us
    dot_general x11 -> x0, matrix products: 35.9 us -> none  [the longest x1 6.65 us: per_device(): jnp.dot(down_slice[:, :adapter_rank], query_delta, preferred_element_type...]
    psum x1 -> x0, blocking collectives: 23.2 us -> none  [per_device(): attended = lax.psum(partial_out, 'tensor').astype(jnp.bfloat16)]
    slice x1 -> x0, local copies, waits for them, and re-layouts: 6.02 us -> none  [per_device(): key_value_cache[1]]
    all_gather x1 -> x0, local copies, waits for them, and re-layouts: 4.45 us -> none  [per_device(): lax.all_gather(adapter_down, ('learner', 'tensor'), axis=0, tiled=True)]
    add x8 -> x0, other arithmetic: 3.74 us -> none  [the longest x3 3.64 us: combine_pair(): former[2] * former_scale[..., None] + latter[2] * latter_scale[..., None]]
  transfers between devices with their start and end apart: 2 -> 0, of which waited for: 1 -> 0; matrix products, arithmetic and copies ran while one was open for 17% -> 0% of each run, Pallas kernels for 0% -> 0%
where the time goes in v1:
time: 73.1 us; the launch traced here: 72.6 us
  Pallas kernels  64.6 us (88%)
  local copies, waits for them, and re-layouts  7.28 us (10%)
    pallas_call x1, Pallas kernels, fused_device(): pl.pallas_call(decode_kernel, out_shape=shape(hidden.shape, bf16), in_spe...  28.5 us
    pallas_call x1, Pallas kernels, fused_device(): pl.pallas_call(gather_kernel, out_shape=[shape((16, packed, 128), bf16),...  22.7 us
    pallas_call x1, Pallas kernels, fused_device(): pl.pallas_call(merge_kernel, grid=(steps,), out_shape=[shape(query_base_w...  13.4 us
    unnamed x12, local copies, waits for them, and re-layouts  6.57 us

profile of v1, /device:TPU:0, one launch (start us, length us, event | category | flops | bytes accessed | tf_op | source)
XLA Modules:
  0.0 72.6 jit_solution(13448317388946353939)
XLA Ops:
  0.6 0.7 reshape.9.gain_ref
  1.3 1.0 %copy.13.down_ref = bf16[320,192]{1,0:T(8,128)(2,1)S(1)} copy(bf16[320,192]{0,1:T(8,128)(2,1)} %param.17) | data formatting | bytes 245760 | tf_op args[7]
  2.4 0.0 copy-start.1
  2.4 0.9 %copy-done.1 = bf16[2,8,5120]{2,1,0:T(8,128)(2,1)S(1)} copy-done((bf16[2,8,5120]{2,1,0:T(8,128)(2,1)S(1)}, bf16[2,8,5120]{2,1,0:T(8,128)(2,1)}, u32[]{:S(2)}) %copy-start.1) | copy-done | bytes 163864
  3.3 0.0 copy-start.2
  3.3 0.8 %copy-done.2 = bf16[16,1024]{1,0:T(8,128)(2,1)S(1)} copy-done((bf16[16,1024]{1,0:T(8,128)(2,1)S(1)}, bf16[16,1024]{1,0:T(8,128)(2,1)}, u32[]{:S(2)}) %copy-start.2) | copy-done | bytes 32792
  4.1 0.0 copy-start.3
  4.1 0.7 copy-done.3
  4.8 22.7 %gather.1 = (bf16[16,480,128]{2,1,0:T(8,128)(2,1)S(1)}, bf16[128,1024]{1,0:T(8,128)(2,1)S(1)}, bf16[128,256]{1,0:T(8,128)(2,1)S(1)}, bf16[128,256]{1,0:T(8,128)(2,1)S(1)}, bf16[8,16,640]{2,1,0:T(8,128)(2,1)S(1)}) custom-call(bf16[2,8,5120]{2,1,0:T(8,128)(2,1)S(1)} %copy-done.1, bf16[1,5120]{1,0:T(2,128)(2,1)S(1)} %reshape.9.gain_ref, ...), custom_call_target="tpu_custom_call" | custom-call | tf_op jit(solution)/shard_map/gather/pallas_call | solution.py:518
  27.5 0.0 copy-start
  27.5 2.5 %copy-done = bf16[2,5120,256]{2,1,0:T(8,128)(2,1)S(1)} copy-done((bf16[2,5120,256]{2,1,0:T(8,128)(2,1)S(1)}, bf16[2,5120,256]{2,1,0:T(8,128)(2,1)}, u32[]{:S(2)}) %copy-start) | copy-done | bytes 5242904
  30.0 0.0 copy-start.4
  30.0 13.4 %merge.1 = (bf16[5120,1024]{1,0:T(8,128)(2,1)}, bf16[2,5120,256]{2,1,0:T(8,128)(2,1)}, f32[16,1024]{1,0:T(8,128)S(1)}, f32[16,256]{1,0:T(8,128)S(1)}, f32[16,256]{1,0:T(8,128)S(1)}) custom-call(bf16[16,480,128]{2,1,0:T(8,128)(2,1)S(1)} %get-tuple-element.13.p_ref, bf16[128,1024]{1,0:T(8,128)(2,1)S(1)} %get-tuple-element.14.uq_ref, ...), custom_call_target="tpu_custom_call" | custom-call | tf_op jit(solution)/shard_map/merge/pallas_call | solution.py:537
  43.3 0.0 copy-done.4
  43.3 28.5 %decode.1 = bf16[2,8,5120]{2,1,0:T(8,128)(2,1)S(1)} custom-call(s32[8]{0:T(128)S(1)} %copy-done.4, f32[16,1024]{1,0:T(8,128)S(1)} %get-tuple-element.18.qs_ref, f32[16,256]{1,0:T(8,128)S(1)} %get-tuple-element.19.ks_ref, f32[16,256]{1,0:T(8,128)S(1)} %get-tuple-element.20.vs_ref, bf16[2,8,256,1024]{3,2,1,0:T(8,128)(2,1)} %cache_hbm.1, bf16[1024,5120]{1,0:T(8,128)(2,1)} %wo_hbm.1), custom_call_target="tpu_custom_call" | custom-call | tf_op jit(solution)/shard_map/decode/pallas_call | solution.py:559
  71.9 0.7 copy.15
Async XLA Ops:
  2.4 0.9 %copy-start.1 = (bf16[2,8,5120]{2,1,0:T(8,128)(2,1)S(1)}, bf16[2,8,5120]{2,1,0:T(8,128)(2,1)}, u32[]{:S(2)}) copy-start(bf16[2,8,5120]{2,1,0:T(8,128)(2,1)} %hidden_ref.1) | copy-start | bytes 491524
  3.3 0.8 %copy-start.2 = (bf16[16,1024]{1,0:T(8,128)(2,1)S(1)}, bf16[16,1024]{1,0:T(8,128)(2,1)}, u32[]{:S(2)}) copy-start(bf16[16,1024]{1,0:T(8,128)(2,1)} %upq_ref.1) | copy-start | bytes 98308
  4.1 0.7 copy-start.3
  27.5 2.5 %copy-start = (bf16[2,5120,256]{2,1,0:T(8,128)(2,1)S(1)}, bf16[2,5120,256]{2,1,0:T(8,128)(2,1)}, u32[]{:S(2)}) copy-start(bf16[2,5120,256]{2,1,0:T(8,128)(2,1)} %wkv_ref.1) | copy-start | bytes 15728644
  30.0 13.4 %copy-start.4 = (s32[8]{0:T(128)S(1)}, s32[8]{0:T(128)}, u32[]{:S(2)}) copy-start(s32[8]{0:T(128)} %lengths_ref.1) | copy-start | bytes 100

commit v2 on v1

--- a/solution.py
+++ b/solution.py
@@ -198,9 +198,9 @@
 
 
 def gather_kernel(
-    hidden_ref, gain_ref, down_ref, upq_ref, upkv_ref,
-    pall_ref, uq_ref, uk_ref, uv_ref, nb_ref,
-    pk, upq_g, upkv_g, up_send, up_recv, b_send, b_recv, own_sem,
+    hidden_hbm, gain_ref, down_ref, upq_ref, upkv_ref, wq_hbm, wkv_hbm, cache_hbm,
+    pall_ref, uq_ref, uk_ref, uv_ref, nb_ref, wq_out, wkv_out, cache_out,
+    pk, upq_g, upkv_g, hidden_ref, up_send, up_recv, b_send, b_recv, own_sem, load_sem,
 ):
     f32, bf16 = jnp.float32, jnp.bfloat16
     L, T = 4, 4
@@ -211,6 +211,16 @@
     for d in range(1, 4):
         pl.semaphore_signal(barrier, inc=1, device_id={"tensor": tp[d]}, device_id_type=MESH)
         pl.semaphore_signal(barrier, inc=1, device_id={"learner": lp[d]}, device_id_type=MESH)
+    hload = pltpu.make_async_copy(hidden_hbm, hidden_ref, load_sem.at[0])
+    hload.start()
+    locals_ = [
+        pltpu.make_async_copy(upq_ref, upq_g.at[l], load_sem.at[1]),
+        pltpu.make_async_copy(upkv_ref, upkv_g.at[l], load_sem.at[2]),
+    ]
+    for k, (src, dst) in enumerate(
+        ((wq_hbm, wq_out), (wkv_hbm, wkv_out), (cache_hbm, cache_out))
+    ):
+        locals_.append(pltpu.make_async_copy(src, dst, load_sem.at[3 + k]))
     shard = down_ref[...]
     rows = shard.shape[0]
     half = rows // 2
@@ -255,10 +265,11 @@
             )
             c.start()
             ups.append(c)
-    upq_g[l] = upq_ref[...]
-    upkv_g[l] = upkv_ref[...]
+    for c in locals_:
+        c.start()
 
     model = gain_ref.shape[1]
+    hload.wait()
     wide = hidden_ref[...].astype(f32).reshape(16, model)
     inv = lax.rsqrt(jnp.mean(wide * wide, -1, keepdims=True) + NORM_EPSILON)
     normed = (wide * inv * gain_ref[...].astype(f32)).astype(bf16)
@@ -279,6 +290,8 @@
         bulk(pall_ref.at[blk], blk, {"learner": l1})
     for c in ups:
         c.wait_recv()
+    for c in locals_[:2]:
+        c.wait()
     uq_ref[0:64, :] = upq_g[...].reshape(64, upq_g.shape[2])
     kvg = upkv_g[...]
     uk_ref[64:128, :] = kvg[:, 0].reshape(64, upkv_g.shape[3])
@@ -290,6 +303,8 @@
         arrived(l1 * T + k)
         arrived(l3 * T + k)
     own.wait()
+    for c in locals_[2:]:
+        c.wait()
     for c in ups + waits:
         c.wait_send()
 
@@ -328,12 +343,11 @@
 
 
 def decode_kernel(
-    lengths_ref, qs_ref, ks_ref, vs_ref, cache_hbm, wo_hbm,
+    lengths_ref, qs_ref, ks_ref, vs_ref, cache, wo,
     att_ref,
-    kc, vc, wo,
     qtmp, qall, keyf, valf, nsend, nrecv, msend, mrecv, res, abuf,
     psend, precv, asend, arecv,
-    load_sem, q_send, q_recv, n_send, n_recv, m_send, m_recv, p_send, p_recv, a_send, a_recv,
+    q_send, q_recv, n_send, n_recv, m_send, m_recv, p_send, p_recv, a_send, a_recv,
 ):
     f32, bf16 = jnp.float32, jnp.bfloat16
     T = 4
@@ -348,13 +362,6 @@
     barrier = pltpu.get_barrier_semaphore()
     for d in range(1, 4):
         pl.semaphore_signal(barrier, inc=1, device_id=to_t(d), device_id_type=MESH)
-    loads = [
-        pltpu.make_async_copy(cache_hbm.at[0], kc, load_sem.at[0]),
-        pltpu.make_async_copy(cache_hbm.at[1], vc, load_sem.at[1]),
-        pltpu.make_async_copy(wo_hbm, wo, load_sem.at[2]),
-    ]
-    for c in loads:
-        c.start()
     waits = []
 
     def send(src, dst, ssem, rsem, dev):
@@ -395,10 +402,8 @@
     for h in range(2):
         keyf[:, h * 128 : (h + 1) * 128] = rope(kacc[:, h * 128 : (h + 1) * 128]).astype(bf16).astype(f32)
 
-    loads[0].wait()
-    loads[1].wait()
     first = sub[:, 0:1] < 8
-    place = t * kc.shape[1] + lax.broadcasted_iota(jnp.int32, (16, kc.shape[1]), 1)
+    place = t * cache.shape[2] + lax.broadcasted_iota(jnp.int32, (16, cache.shape[2]), 1)
     lane2 = lane
     ns_copies = [None] * 4
     per = 4
@@ -411,8 +416,8 @@
             for u in range(per):
                 r = i * per + u
                 q16 = qall[d, pl.ds(pl.multiple_of(r * 16, 16), 16), :]
-                kk = kc[r, :, pl.ds(cols, 256)]
-                vv = vc[r, :, pl.ds(cols, 256)]
+                kk = cache[0, r, :, pl.ds(cols, 256)]
+                vv = cache[1, r, :, pl.ds(cols, 256)]
                 dims = (((1,), (1,)), ((), ()))
                 s0 = lax.dot_general(q16, kk[:, :128], dims, preferred_element_type=f32)
                 s1 = lax.dot_general(q16, kk[:, 128:], dims, preferred_element_type=f32)
@@ -475,7 +480,6 @@
             abuf[s * 8 : (s + 1) * 8, h * 128 : (h + 1) * 128] = res[pl.ds(start, 8, stride=16), :]
     a = abuf[...].astype(bf16)
 
-    loads[2].wait()
     quarter = model // T
     ps = []
     for d in (2, 1, 3):
@@ -515,23 +519,26 @@
     dma = pltpu.SemaphoreType.DMA
     spec = lambda m: pl.BlockSpec(memory_space=m)
     shape = jax.ShapeDtypeStruct
-    p_all, uq, uk, uv, blocks = pl.pallas_call(
+    p_all, uq, uk, uv, blocks, wq_v, wkv_v, cache_v = pl.pallas_call(
         gather_kernel,
         out_shape=[
             shape((16, packed, 128), bf16), shape((128, 1024), bf16), shape((128, 256), bf16),
             shape((128, 256), bf16), shape((steps, 16, model // steps), bf16),
+            shape(query_base_weight.shape, bf16), shape(key_value_weight.shape, bf16),
+            shape(key_value_cache.shape, bf16),
         ],
-        in_specs=[spec(V)] * 5,
-        out_specs=[spec(A)] + [spec(V)] * 4,
+        in_specs=[spec(A), spec(V), spec(V)] + [spec(A)] * 5,
+        out_specs=[spec(A)] + [spec(V)] * 4 + [spec(A)] * 3,
         scratch_shapes=[
-            V((packed, 128), bf16), V((4, 16, 1024), bf16), V((4, 2, 16, 256), bf16),
-            dma((2, 4)), dma((2, 4)), dma((15,)), dma((16,)), dma,
+            V((packed, 128), bf16), V((4, 16, 1024), bf16), V((4, 2, 16, 256), bf16), V(hidden.shape, bf16),
+            dma((2, 4)), dma((2, 4)), dma((15,)), dma((16,)), dma, dma((6,)),
         ],
         compiler_params=pltpu.CompilerParams(
-            collective_id=0, has_side_effects=True, vmem_limit_bytes=32 * 1024 * 1024
+            collective_id=0, has_side_effects=True, vmem_limit_bytes=6 * 1024 * 1024
         ),
         name="gather",
-    )(hidden, input_norm_gain.reshape(1, model), adapter_down, query_up_factor, key_value_up)
+    )(hidden, input_norm_gain.reshape(1, model), adapter_down, query_up_factor, key_value_up,
+      query_base_weight, key_value_weight, key_value_cache)
     wide = model // steps
     whole = lambda *sh: pl.BlockSpec(sh, lambda i: (0,) * len(sh))
     merged, kv_merged, qs, ks, vs = pl.pallas_call(
@@ -553,28 +560,26 @@
             pl.BlockSpec((2, wide, 256), lambda i: (0, i, 0)),
             whole(16, 1024), whole(16, 256), whole(16, 256),
         ],
-        compiler_params=pltpu.CompilerParams(vmem_limit_bytes=40 * 1024 * 1024),
+        compiler_params=pltpu.CompilerParams(vmem_limit_bytes=14 * 1024 * 1024),
         name="merge",
-    )(p_all, uq, uk, uv, blocks, query_base_weight, key_value_weight)
+    )(p_all, uq, uk, uv, blocks, wq_v, wkv_v)
     attended = pl.pallas_call(
         decode_kernel,
         out_shape=shape(hidden.shape, bf16),
-        in_specs=[spec(S)] + [spec(V)] * 3 + [spec(A)] * 2,
+        in_specs=[spec(S)] + [spec(V)] * 5,
         out_specs=spec(V),
         scratch_shapes=[
-            V((8, 256, 1024), bf16), V((8, 256, 1024), bf16), V((1024, model), bf16),
             V((128, 128), f32), V((4, 128, 128), bf16), V((16, 256), f32), V((16, 256), f32),
             V((4, 128, 128), bf16), V((4, 128, 128), bf16), V((4, 16, 128), f32), V((4, 16, 128), f32),
             V((128, 128), f32), V((16, 1024), f32),
             V((4, 16, part), bf16), V((4, 16, part), bf16), V((16, part), bf16), V((4, 16, part), bf16),
-            dma((3,)),
         ]
         + [dma((4,))] * 10,
         compiler_params=pltpu.CompilerParams(
-            collective_id=1, has_side_effects=True, vmem_limit_bytes=48 * 1024 * 1024
+            collective_id=1, has_side_effects=True, vmem_limit_bytes=10 * 1024 * 1024
         ),
         name="decode",
-    )(lengths, qs, ks, vs, key_value_cache, output_weight)
+    )(lengths, qs, ks, vs, cache_v, output_weight)
     return attended, merged, kv_merged
 
 

time: 73.1 us -> 71.2 us (0.974)
  Pallas kernels: 64.6 us -> 59.5 us
  local copies, waits for them, and re-layouts: 7.28 us -> 10.7 us
    pallas_call x1, Pallas kernels: 13.4 us -> 9.32 us  [fused_device(): pl.pallas_call(merge_kernel, grid=(steps,), out_shape=[shape(query_base_w...]
    unnamed x12 -> x16, local copies, waits for them, and re-layouts: 6.57 us -> 9.96 us
    pallas_call x1, Pallas kernels: 28.5 us -> 27.4 us  [fused_device(): pl.pallas_call(decode_kernel, out_shape=shape(hidden.shape, bf16), in_spe...]
where the time goes in v2:
time: 71.2 us; the launch traced here: 70.8 us
  Pallas kernels  59.5 us (84%)
  local copies, waits for them, and re-layouts  10.7 us (15%)
    pallas_call x1, Pallas kernels, fused_device(): pl.pallas_call(decode_kernel, out_shape=shape(hidden.shape, bf16), in_spe...  27.4 us
    pallas_call x1, Pallas kernels, fused_device(): pl.pallas_call(gather_kernel, out_shape=[shape((16, packed, 128), bf16),...  22.7 us
    unnamed x16, local copies, waits for them, and re-layouts  9.96 us
    pallas_call x1, Pallas kernels, fused_device(): pl.pallas_call(merge_kernel, grid=(steps,), out_shape=[shape(query_base_w...  9.32 us

profile of v2, /device:TPU:0, one launch (start us, length us, event | category | flops | bytes accessed | tf_op | source)
XLA Modules:
  0.0 70.8 jit_solution(8992304312237958587)
XLA Ops:
  0.6 0.7 %reshape.9.gain_ref = bf16[1,5120]{1,0:T(2,128)(2,1)S(1)} reshape(bf16[5120]{0:T(1024)(128)(2,1)} %param.11) | data formatting | bytes 20480 | tf_op jit(solution)/shard_map/reshape | solution.py:540
  1.3 1.0 %copy.13.down_ref = bf16[320,192]{1,0:T(8,128)(2,1)S(1)} copy(bf16[320,192]{0,1:T(8,128)(2,1)} %param.17) | data formatting | bytes 245760 | tf_op args[7]
  2.4 0.0 copy-start.1
  2.4 3.4 %copy-done.1 = bf16[2,8,256,1024]{3,2,1,0:T(8,128)(2,1)S(1)} copy-done((bf16[2,8,256,1024]{3,2,1,0:T(8,128)(2,1)S(1)}, bf16[2,8,256,1024]{3,2,1,0:T(8,128)(2,1)}, u32[]{:S(2)}) %copy-start.1) | copy-done | bytes 8388632
  5.8 0.0 copy-start.2
  5.8 2.5 %copy-done.2 = bf16[2,5120,256]{2,1,0:T(8,128)(2,1)S(1)} copy-done((bf16[2,5120,256]{2,1,0:T(8,128)(2,1)S(1)}, bf16[2,5120,256]{2,1,0:T(8,128)(2,1)}, u32[]{:S(2)}) %copy-start.2) | copy-done | bytes 5242904
  8.3 0.0 copy-start.3
  8.3 0.9 %copy-done.3 = bf16[2,8,5120]{2,1,0:T(8,128)(2,1)S(1)} copy-done((bf16[2,8,5120]{2,1,0:T(8,128)(2,1)S(1)}, bf16[2,8,5120]{2,1,0:T(8,128)(2,1)}, u32[]{:S(2)}) %copy-start.3) | copy-done | bytes 163864
  9.2 0.0 copy-start.4
  9.2 0.8 %copy-done.4 = bf16[16,1024]{1,0:T(8,128)(2,1)S(1)} copy-done((bf16[16,1024]{1,0:T(8,128)(2,1)S(1)}, bf16[16,1024]{1,0:T(8,128)(2,1)}, u32[]{:S(2)}) %copy-start.4) | copy-done | bytes 32792
  9.9 0.0 copy-start.5
  9.9 0.7 %copy-done.5 = bf16[2,16,256]{2,1,0:T(8,128)(2,1)S(1)} copy-done((bf16[2,16,256]{2,1,0:T(8,128)(2,1)S(1)}, bf16[2,16,256]{2,1,0:T(8,128)(2,1)}, u32[]{:S(2)}) %copy-start.5) | copy-done | bytes 16408
  10.6 22.7 %gather.1 = (bf16[16,480,128]{2,1,0:T(8,128)(2,1)S(1)}, bf16[128,1024]{1,0:T(8,128)(2,1)S(1)}, bf16[128,256]{1,0:T(8,128)(2,1)S(1)}, bf16[128,256]{1,0:T(8,128)(...) custom-call(bf16[2,8,5120]{2,1,0:T(8,128)(2,1)S(1)} %copy-done.3, ...), custom_call_target="tpu_custom_call" | custom-call | tf_op jit(solution)/shard_map/gather/pallas_call | solution.py:522
  33.4 0.0 copy-start
  33.4 0.0 copy-start.6
  33.4 9.3 %merge.1 = (bf16[5120,1024]{1,0:T(8,128)(2,1)}, bf16[2,5120,256]{2,1,0:T(8,128)(2,1)}, f32[16,1024]{1,0:T(8,128)S(1)}, f32[16,256]{1,0:T(8,128)S(1)}, f32[16,256]{1,0:T(8,128)S(1)}) custom-call(bf16[16,480,128]{2,1,0:T(8,128)(2,1)S(1)} %get-tuple-element.16.p_ref, bf16[128,1024]{1,0:T(8,128)(2,1)S(1)} %get-tuple-element.17.uq_ref, ...), custom_call_target="tpu_custom_call" | custom-call | tf_op jit(solution)/shard_map/merge/pallas_call | solution.py:544
  42.7 0.0 copy-done
  42.7 0.0 copy-done.6
  42.8 27.4 %decode.1 = bf16[2,8,5120]{2,1,0:T(8,128)(2,1)S(1)} custom-call(s32[8]{0:T(128)S(1)} %copy-done.6, f32[16,1024]{1,0:T(8,128)S(1)} %get-tuple-element.23.qs_ref, f32[16,256]{1,0:T(8,128)S(1)} %get-tuple-element.24.ks_ref, f32[16,256]{1,0:T(8,128)S(1)} %get-tuple-element.25.vs_ref, bf16[2,8,256,1024]{3,2,1,0:T(8,128)(2,1)S(1)} %get-tuple-element.26.cache, ...), custom_call_target="tpu_custom_call" | custom-call | tf_op jit(solution)/shard_map/decode/pallas_call | solution.py:566
  70.1 0.7 copy.15
Async XLA Ops:
  2.4 3.4 %copy-start.1 = (bf16[2,8,256,1024]{3,2,1,0:T(8,128)(2,1)S(1)}, bf16[2,8,256,1024]{3,2,1,0:T(8,128)(2,1)}, u32[]{:S(2)}) copy-start(bf16[2,8,256,1024]{3,2,1,0:T(8,128)(2,1)} %cache_hbm.1) | copy-start | bytes 25165828
  5.8 2.5 %copy-start.2 = (bf16[2,5120,256]{2,1,0:T(8,128)(2,1)S(1)}, bf16[2,5120,256]{2,1,0:T(8,128)(2,1)}, u32[]{:S(2)}) copy-start(bf16[2,5120,256]{2,1,0:T(8,128)(2,1)} %wkv_hbm.1) | copy-start | bytes 15728644
  8.3 0.9 %copy-start.3 = (bf16[2,8,5120]{2,1,0:T(8,128)(2,1)S(1)}, bf16[2,8,5120]{2,1,0:T(8,128)(2,1)}, u32[]{:S(2)}) copy-start(bf16[2,8,5120]{2,1,0:T(8,128)(2,1)} %hidden_hbm.1) | copy-start | bytes 491524
  9.2 0.8 %copy-start.4 = (bf16[16,1024]{1,0:T(8,128)(2,1)S(1)}, bf16[16,1024]{1,0:T(8,128)(2,1)}, u32[]{:S(2)}) copy-start(bf16[16,1024]{1,0:T(8,128)(2,1)} %upq_ref.1) | copy-start | bytes 98308
  9.9 0.7 %copy-start.5 = (bf16[2,16,256]{2,1,0:T(8,128)(2,1)S(1)}, bf16[2,16,256]{2,1,0:T(8,128)(2,1)}, u32[]{:S(2)}) copy-start(bf16[2,16,256]{2,1,0:T(8,128)(2,1)} %upkv_ref.1) | copy-start | bytes 49156
  33.4 9.3 %copy-start = (bf16[1024,5120]{1,0:T(8,128)(2,1)S(1)}, bf16[1024,5120]{1,0:T(8,128)(2,1)}, u32[]{:S(2)}) copy-start(bf16[1024,5120]{1,0:T(8,128)(2,1)} %wo.1) | copy-start | bytes 31457284
  33.4 9.3 %copy-start.6 = (s32[8]{0:T(128)S(1)}, s32[8]{0:T(128)}, u32[]{:S(2)}) copy-start(s32[8]{0:T(128)} %lengths_ref.1) | copy-start | bytes 100

commit v3 on v2

--- a/solution.py
+++ b/solution.py
@@ -406,7 +406,7 @@
     place = t * cache.shape[2] + lax.broadcasted_iota(jnp.int32, (16, cache.shape[2]), 1)
     lane2 = lane
     ns_copies = [None] * 4
-    per = 4
+    per = 8
 
     def attend(d):
         owner = lax.rem(t + T - d, T)

time: 71.2 us -> 70.6 us (level)
  no operation moved by 1% of the time
where the time goes in v3:
time: 70.6 us; the launch traced here: 70.2 us
  Pallas kernels  58.8 us (83%)
  local copies, waits for them, and re-layouts  10.7 us (15%)
    pallas_call x1, Pallas kernels, fused_device(): pl.pallas_call(decode_kernel, out_shape=shape(hidden.shape, bf16), in_spe...  26.7 us
    pallas_call x1, Pallas kernels, fused_device(): pl.pallas_call(gather_kernel, out_shape=[shape((16, packed, 128), bf16),...  22.7 us
    unnamed x16, local copies, waits for them, and re-layouts  9.96 us
    pallas_call x1, Pallas kernels, fused_device(): pl.pallas_call(merge_kernel, grid=(steps,), out_shape=[shape(query_base_w...  9.32 us

profile of v3, /device:TPU:0, one launch (start us, length us, event | category | flops | bytes accessed | tf_op | source)
XLA Modules:
  0.0 70.2 jit_solution(7084030545732088777)
XLA Ops:
  0.6 0.7 %reshape.9.gain_ref = bf16[1,5120]{1,0:T(2,128)(2,1)S(1)} reshape(bf16[5120]{0:T(1024)(128)(2,1)} %param.11) | data formatting | bytes 20480 | tf_op jit(solution)/shard_map/reshape | solution.py:540
  1.3 1.0 %copy.13.down_ref = bf16[320,192]{1,0:T(8,128)(2,1)S(1)} copy(bf16[320,192]{0,1:T(8,128)(2,1)} %param.17) | data formatting | bytes 245760 | tf_op args[7]
  2.4 0.0 copy-start.1
  2.4 3.4 %copy-done.1 = bf16[2,8,256,1024]{3,2,1,0:T(8,128)(2,1)S(1)} copy-done((bf16[2,8,256,1024]{3,2,1,0:T(8,128)(2,1)S(1)}, bf16[2,8,256,1024]{3,2,1,0:T(8,128)(2,1)}, u32[]{:S(2)}) %copy-start.1) | copy-done | bytes 8388632
  5.8 0.0 copy-start.2
  5.8 2.5 %copy-done.2 = bf16[2,5120,256]{2,1,0:T(8,128)(2,1)S(1)} copy-done((bf16[2,5120,256]{2,1,0:T(8,128)(2,1)S(1)}, bf16[2,5120,256]{2,1,0:T(8,128)(2,1)}, u32[]{:S(2)}) %copy-start.2) | copy-done | bytes 5242904
  8.3 0.0 copy-start.3
  8.3 0.9 %copy-done.3 = bf16[2,8,5120]{2,1,0:T(8,128)(2,1)S(1)} copy-done((bf16[2,8,5120]{2,1,0:T(8,128)(2,1)S(1)}, bf16[2,8,5120]{2,1,0:T(8,128)(2,1)}, u32[]{:S(2)}) %copy-start.3) | copy-done | bytes 163864
  9.2 0.0 copy-start.4
  9.2 0.8 %copy-done.4 = bf16[16,1024]{1,0:T(8,128)(2,1)S(1)} copy-done((bf16[16,1024]{1,0:T(8,128)(2,1)S(1)}, bf16[16,1024]{1,0:T(8,128)(2,1)}, u32[]{:S(2)}) %copy-start.4) | copy-done | bytes 32792
  9.9 0.0 copy-start.5
  9.9 0.7 %copy-done.5 = bf16[2,16,256]{2,1,0:T(8,128)(2,1)S(1)} copy-done((bf16[2,16,256]{2,1,0:T(8,128)(2,1)S(1)}, bf16[2,16,256]{2,1,0:T(8,128)(2,1)}, u32[]{:S(2)}) %copy-start.5) | copy-done | bytes 16408
  10.6 22.7 %gather.1 = (bf16[16,480,128]{2,1,0:T(8,128)(2,1)S(1)}, bf16[128,1024]{1,0:T(8,128)(2,1)S(1)}, bf16[128,256]{1,0:T(8,128)(2,1)S(1)}, bf16[128,256]{1,0:T(8,128)(...) custom-call(bf16[2,8,5120]{2,1,0:T(8,128)(2,1)S(1)} %copy-done.3, ...), custom_call_target="tpu_custom_call" | custom-call | tf_op jit(solution)/shard_map/gather/pallas_call | solution.py:522
  33.4 0.0 copy-start
  33.4 0.0 copy-start.6
  33.4 9.3 %merge.1 = (bf16[5120,1024]{1,0:T(8,128)(2,1)}, bf16[2,5120,256]{2,1,0:T(8,128)(2,1)}, f32[16,1024]{1,0:T(8,128)S(1)}, f32[16,256]{1,0:T(8,128)S(1)}, f32[16,256]{1,0:T(8,128)S(1)}) custom-call(bf16[16,480,128]{2,1,0:T(8,128)(2,1)S(1)} %get-tuple-element.16.p_ref, bf16[128,1024]{1,0:T(8,128)(2,1)S(1)} %get-tuple-element.17.uq_ref, ...), custom_call_target="tpu_custom_call" | custom-call | tf_op jit(solution)/shard_map/merge/pallas_call | solution.py:544
  42.7 0.0 copy-done
  42.7 0.0 copy-done.6
  42.8 26.7 %decode.1 = bf16[2,8,5120]{2,1,0:T(8,128)(2,1)S(1)} custom-call(s32[8]{0:T(128)S(1)} %copy-done.6, f32[16,1024]{1,0:T(8,128)S(1)} %get-tuple-element.23.qs_ref, f32[16,256]{1,0:T(8,128)S(1)} %get-tuple-element.24.ks_ref, f32[16,256]{1,0:T(8,128)S(1)} %get-tuple-element.25.vs_ref, bf16[2,8,256,1024]{3,2,1,0:T(8,128)(2,1)S(1)} %get-tuple-element.26.cache, ...), custom_call_target="tpu_custom_call" | custom-call | tf_op jit(solution)/shard_map/decode/pallas_call | solution.py:566
  69.5 0.7 copy.15
Async XLA Ops:
  2.4 3.4 %copy-start.1 = (bf16[2,8,256,1024]{3,2,1,0:T(8,128)(2,1)S(1)}, bf16[2,8,256,1024]{3,2,1,0:T(8,128)(2,1)}, u32[]{:S(2)}) copy-start(bf16[2,8,256,1024]{3,2,1,0:T(8,128)(2,1)} %cache_hbm.1) | copy-start | bytes 25165828
  5.8 2.5 %copy-start.2 = (bf16[2,5120,256]{2,1,0:T(8,128)(2,1)S(1)}, bf16[2,5120,256]{2,1,0:T(8,128)(2,1)}, u32[]{:S(2)}) copy-start(bf16[2,5120,256]{2,1,0:T(8,128)(2,1)} %wkv_hbm.1) | copy-start | bytes 15728644
  8.3 0.9 %copy-start.3 = (bf16[2,8,5120]{2,1,0:T(8,128)(2,1)S(1)}, bf16[2,8,5120]{2,1,0:T(8,128)(2,1)}, u32[]{:S(2)}) copy-start(bf16[2,8,5120]{2,1,0:T(8,128)(2,1)} %hidden_hbm.1) | copy-start | bytes 491524
  9.2 0.8 %copy-start.4 = (bf16[16,1024]{1,0:T(8,128)(2,1)S(1)}, bf16[16,1024]{1,0:T(8,128)(2,1)}, u32[]{:S(2)}) copy-start(bf16[16,1024]{1,0:T(8,128)(2,1)} %upq_ref.1) | copy-start | bytes 98308
  9.9 0.7 %copy-start.5 = (bf16[2,16,256]{2,1,0:T(8,128)(2,1)S(1)}, bf16[2,16,256]{2,1,0:T(8,128)(2,1)}, u32[]{:S(2)}) copy-start(bf16[2,16,256]{2,1,0:T(8,128)(2,1)} %upkv_ref.1) | copy-start | bytes 49156
  33.4 9.3 %copy-start = (bf16[1024,5120]{1,0:T(8,128)(2,1)S(1)}, bf16[1024,5120]{1,0:T(8,128)(2,1)}, u32[]{:S(2)}) copy-start(bf16[1024,5120]{1,0:T(8,128)(2,1)} %wo.1) | copy-start | bytes 31457284
  33.4 9.3 %copy-start.6 = (s32[8]{0:T(128)S(1)}, s32[8]{0:T(128)}, u32[]{:S(2)}) copy-start(s32[8]{0:T(128)} %lengths_ref.1) | copy-start | bytes 100
